TPU v7x, 512 devices: a whole 4x4x16 slice. The times are simulated.
512 devices in a mesh: row: 8 (over y, z_hi), col: 64 (over z_lo, x, core).
Axes of the slice: x: 4, y: 4, z: 16 (z_hi: 2, z_lo: 8; z = z_hi * 8 + z_lo), core: 2. Of those that a mesh axis runs over, the one named last changes fastest.
Arguments:
- side_a: float32 [64, 8192], P('row', 'col'), may hold values from -6 to 6
- side_b: float32 [2048, 8192], P('col', 'row'), may hold values from -6 to 6
- pair_grad: float32 [64, 2048, 128], P('row', 'col'), may hold values from -6 to 6
- out_weight: float32 [1024, 128], replicated, may hold values from -0.1875 to 0.1875
Outputs:
- grad_a: float32 [64, 8192], P('row', 'col')
- grad_b: float32 [2048, 8192], P('col', 'row')
- grad_weight: float32 [1024, 128], replicated
- grad_bias: float32 [128], replicated
All inputs are finite; a program needn't handle non-finite values.
Results may differ from a plain program's by a relative error of at most 0.00013.
Values sent between devices are 32-bit elements; how exact they have to be, the bound alone decides.
A program may use at most 64 MiB of HBM per device.

v0:
```python
import jax
import jax.numpy as jnp
from jax import lax
from jax.sharding import PartitionSpec as P

S = 256
C = 32
P_SIZE = 128


def local(side_a, side_b, pair_grad, out_weight):
    high = lax.Precision.HIGHEST
    rows = pair_grad.shape[0]
    cols = pair_grad.shape[1]
    left = lax.all_gather(side_a, "col", axis=1, tiled=True).reshape(rows, S, C)
    right = lax.all_gather(side_b, "row", axis=1, tiled=True).reshape(cols, S, C)
    left_flat = jnp.transpose(left, (0, 2, 1)).reshape(rows * C, S)
    right_flat = jnp.transpose(right, (1, 0, 2)).reshape(S, cols * C)
    flat_pair = pair_grad.reshape(rows * cols, P_SIZE)
    grad_outer = jnp.dot(flat_pair, out_weight.T, precision=high)
    grad_tile = jnp.transpose(grad_outer.reshape(rows, cols, C, C), (0, 2, 1, 3)).reshape(
        rows * C, cols * C
    )
    left_grad = jnp.dot(grad_tile, right_flat.T, precision=high) / S
    left_part = jnp.transpose(left_grad.reshape(rows, C, S), (0, 2, 1)).reshape(rows, S * C)
    right_grad = jnp.dot(left_flat.T, grad_tile, precision=high) / S
    right_part = jnp.transpose(right_grad.reshape(S, cols, C), (1, 0, 2)).reshape(cols, S * C)
    left_total = lax.psum(left_part, "col")
    right_total = lax.psum(right_part, "row")
    left_width = side_a.shape[1]
    right_width = side_b.shape[1]
    grad_a = lax.dynamic_slice_in_dim(left_total, lax.axis_index("col") * left_width, left_width, 1)
    grad_b = lax.dynamic_slice_in_dim(
        right_total, lax.axis_index("row") * right_width, right_width, 1
    )
    outer = jnp.dot(left_flat, right_flat, precision=high) / S
    outer = jnp.transpose(outer.reshape(rows, C, cols, C), (0, 2, 1, 3)).reshape(rows * cols, C * C)
    weight_part = jnp.dot(outer.T, flat_pair, precision=high)
    bias_part = jnp.sum(flat_pair, axis=0)
    weight_sums = lax.psum((weight_part, bias_part), ("row", "col"))
    return (grad_a, grad_b, weight_sums[0], weight_sums[1])


def solution(mesh):
    in_specs = (P("row", "col"), P("col", "row"), P("row", "col", None), P())
    out_specs = (P("row", "col"), P("col", "row"), P(), P())
    return jax.shard_map(local, mesh=mesh, in_specs=in_specs, out_specs=out_specs, check_vma=False)
```

profile of v0, /device:TPU:1, one launch (start us, length us, event | category | flops | bytes accessed | tf_op | source)
XLA Modules:
  0.0 1648.2 jit_solution(14450162567662222692)
XLA Ops:
  7.2 0.0 copy-start
  7.2 0.0 all-gather.2.cloned.1.call-start
  7.2 0.7 all-gather.2.cloned.1.call-update
  7.9 0.0 all-reduce.6.cloned.1.call-start
  8.0 0.3 copy-done
  8.2 0.0 copy-start.2
  8.2 5.9 convolution_bitcast_fusion
  14.1 3.7 reshape.48
  17.9 0.0 copy-done.2
  17.9 130.1 %all_gather.7 = f32[8,8192]{1,0:T(8,128)S(1)} all-gather(f32[8,128]{1,0:T(8,128)S(1)} %copy-done.2), channel_id=1, replica_groups=mesh['row'=8,'col'=64] {'col'}, dimensions={1}, use_global_device_ids=true | all-gather | bytes 266240 | tf_op jit(solution)/shard_map/all_gather | solution.py:15
  148.0 0.3 reshape.53
  148.3 0.3 copy.12
  148.7 1.8 convolution_multiply_fusion.1
  150.5 2.6 copy.13
  153.1 4.4 reshape.56
  157.5 0.0 all-reduce.6.cloned.1.call-update
  157.5 0.2 all-reduce.4.cloned.1.call-start
  157.8 0.0 all-gather.2.cloned.1.call-done
  157.8 3.7 reshape.49
  161.5 2.8 copy.10
  164.3 1.0 convolution_multiply_fusion.2
  165.4 0.3 copy.11
  165.7 1.2 reshape.52
  166.9 1.0 convolution_multiply_fusion
  168.0 2.7 reshape.57
  170.7 6.5 copy.17
  177.2 0.0 copy-start.1
  177.2 3.8 reshape.58
  181.0 0.0 all-reduce.4.cloned.1.call-update
  181.0 0.0 all-reduce.8.cloned.1.call-start
  181.1 0.0 copy-done.1
  181.1 2.6 fusion.1
  183.7 0.0 all-reduce.8.cloned.1.call-update
  183.7 0.1 reduce_sum.9
  183.8 148.8 %psum.31 = f32[128]{0:T(128)} all-reduce(f32[128]{0:T(128)S(1)} %reduce_sum.9), channel_id=1, replica_groups=mesh['row'=8,'col'=64] {'row','col'}, use_global_device_ids=true, to_apply=%region_4.0 | all-reduce | flops 128 | bytes 1024 | tf_op jit(solution)/shard_map/psum | solution.py:40
  332.6 57.9 %all-reduce.6.cloned.1.call-done = f32[32,8192]{1,0:T(8,128)} async-done(((f32[32,8192]{1,0:T(8,128)}), f32[32,8192]{1,0:T(8,128)}) %all-reduce.6.cloned.1.call-update) | async-done | bytes 1048592 | tf_op jit(solution)/shard_map/psum | solution.py:29
  390.5 1.6 constant_dynamic-slice_fusion
  392.0 783.0 %all-reduce.4.cloned.1.call-done = f32[8,8192]{1,0:T(8,128)} async-done(((f32[8,8192]{1,0:T(8,128)}), f32[8,8192]{1,0:T(8,128)}) %all-reduce.4.cloned.1.call-update) | async-done | bytes 262160 | tf_op jit(solution)/shard_map/psum | solution.py:28
  1175.0 1.3 constant_dynamic-slice_fusion.1
  1176.3 463.5 %all-reduce.8.cloned.1.call-done = f32[1024,128]{1,0:T(8,128)} async-done(((f32[1024,128]{1,0:T(8,128)}), f32[1024,128]{1,0:T(8,128)}) %all-reduce.8.cloned.1.call-update) | async-done | bytes 524304 | tf_op jit(solution)/shard_map/psum | solution.py:40
  1639.8 1.9 copy.21
Async XLA Ops:
  7.2 1.0 copy-start
  7.2 150.6 %all-gather.2.cloned.1.call-start = ((), (), s32[]{:S(2)}) async-start(), calls=%async_computation | async-start | bytes 1179648 | tf_op jit(solution)/shard_map/all_gather | solution.py:16
  7.9 382.5 %all-reduce.6.cloned.1.call-start = ((), (), s32[]{:S(2)}) async-start(), calls=%async_computation.2 | async-start | bytes 2097152 | tf_op jit(solution)/shard_map/psum | solution.py:29
  8.2 9.7 copy-start.2
  157.5 1017.5 %all-reduce.4.cloned.1.call-start = ((), (), s32[]{:S(2)}) async-start(), calls=%async_computation.1 | async-start | bytes 524288 | tf_op jit(solution)/shard_map/psum | solution.py:28
  177.2 3.9 copy-start.1
  181.0 1458.8 %all-reduce.8.cloned.1.call-start = ((), (), s32[]{:S(2)}) async-start(), calls=%async_computation.3 | async-start | bytes 1048576 | tf_op jit(solution)/shard_map/psum | solution.py:40
Sparse Core Ops, SparseCore 0:
  11.2 95.2 all-gather.1
  157.6 232.7 all-reduce.5
  393.4 781.5 all-reduce.3
  1181.8 457.9 all-reduce.7
where the time goes:
time: 1650 us
  waiting for transfers between devices  1310 us (79%)
  blocking collectives  279 us (17%)
  local copies, waits for them, and re-layouts  37.5 us (2%)
    psum x1, waiting for transfers between devices, local(): left_total = lax.psum(left_part, 'col')  783 us
    psum x1, waiting for transfers between devices, local(): weight_sums = lax.psum((weight_part, bias_part), ('row', 'col'))  464 us
    psum x1, blocking collectives, local(): weight_sums = lax.psum((weight_part, bias_part), ('row', 'col'))  149 us
    all_gather x1, blocking collectives, local(): left = lax.all_gather(side_a, 'col', axis=1, tiled=True).reshape(rows, S, C)  130 us
    psum x1, waiting for transfers between devices, local(): right_total = lax.psum(right_part, 'row')  57.9 us
  transfers between devices with their start and end apart: 4, of which 3 were waited for; matrix products, arithmetic and copies ran while one was open for 3% of the time, Pallas kernels for 0%

commit v1 on v0

v1 whole, which is shorter than its diff:
```python
import jax
import jax.numpy as jnp
from jax import lax
from jax.experimental import pallas as pl
from jax.experimental.pallas import tpu as pltpu
from jax.sharding import PartitionSpec as P

S = 256
C = 32
K = 128
CHUNKS = 4
JC = 32 // CHUNKS
MESH = pl.DeviceIdType.MESH
F32 = jnp.float32
BF16 = jnp.bfloat16

Y_OWN = 0
TWIN = Y_OWN + 3
FWD = TWIN + CHUNKS
A_ONE = FWD + 3 * CHUNKS
A_X = A_ONE + 8
A_CORE = A_X + 3
GA_CORE = A_CORE + 1
GA_X = GA_CORE + 1
GA_Z = GA_X + 3
W_CORE = GA_Z + 8
B_CORE = W_CORE + 1
W_XY = B_CORE + 1
W_Z1 = W_XY + 16
W_Z2 = W_Z1 + 3
W_AG = W_Z2 + 3
W_END = W_AG + 16
N_SEM = W_END + 1

CONTRACT_LANES = (((1,), (1,)), ((), ()))


def high(x):
    return x.astype(BF16).astype(F32)


def kernel(
    a_ref,
    b_ref,
    pg_ref,
    w_ref,
    ga_out,
    gb_out,
    gw_out,
    bias_out,
    g_all,
    a_all,
    ga_all,
    ga_r1,
    ga_r2,
    ga_s,
    ga_r3,
    gw_part,
    gw_r1,
    gw_s,
    gw_r2,
    gw_z1,
    gw_z2,
    bias_own,
    bias_r1,
    t_h,
    t_l,
    u_h,
    u_l,
    wt,
    bs,
    bjs,
    bp,
    bt,
    at1,
    at2,
    ap,
    gi,
    acc_a,
    acc_w,
    send_sem,
    recv_sem,
):
    r = lax.axis_index("row")
    q = lax.axis_index("col")
    y = r // 2
    zh = r % 2
    zl = q // 8
    x = (q // 2) % 4
    core = q % 2
    z = zh * 8 + zl
    place = core * 4 + x
    xy = x * 4 + y

    def dev(y_, z_, x_, core_):
        return (y_ * 2 + z_ // 8, (z_ % 8) * 8 + x_ * 2 + core_)

    def rcopy(src, dst, number, device, arrives=None):
        return pltpu.make_async_remote_copy(
            src_ref=src,
            dst_ref=dst,
            send_sem=send_sem.at[number],
            recv_sem=recv_sem.at[number if arrives is None else arrives],
            device_id=device,
            device_id_type=MESH,
        )

    sibling = dev(y, z, x, 1 - core)
    twin = dev(y, (z + 8) % 16, x, core)
    y_peers = [dev((y + d) % 4, z, x, core) for d in (1, 2, 3)]
    x_peers = [dev(y, z, (x + d) % 4, core) for d in (1, 2, 3)]
    xy_steps = [(dx, dy) for dx in range(4) for dy in range(4) if (dx, dy) != (0, 0)]
    xy_peers = [dev((y + dy) % 4, z, (x + dx) % 4, core) for dx, dy in xy_steps]
    z_near = [dev(y, (z // 4) * 4 + (z + d) % 4, x, core) for d in (1, 2, 3)]
    z_far = [dev(y, (z + 4 * d) % 16, x, core) for d in (1, 2, 3)]
    out_a = [(zl, ((zl + d) % 8) * 8 + x * 2 + core) for d in range(8)]
    in_a = [((r + d) % 8, r * 8 + x * 2 + core) for d in range(8)]
    at_home = zl == r

    barrier = pltpu.get_barrier_semaphore()

    def greet(device):
        pl.semaphore_signal(barrier, inc=1, device_id=device, device_id_type=MESH)

    for device in out_a[1:] + in_a[1:] + z_far + z_near + xy_peers + [sibling]:
        greet(device)

    @pl.when(jnp.logical_not(at_home))
    def _():
        greet(out_a[0])
        greet(in_a[0])

    bias = jnp.zeros((8, K), F32)
    for j in range(32):
        block = pg_ref[pl.ds(j, 8, stride=32), :]
        g_all[r, j] = block
        bias = bias + block
    bias_own[...] = bias

    @pl.when(at_home)
    def _():
        a_all[place, r] = a_ref[...]

    fixed = 14 + 3 + 3 + 15 + 1
    pl.semaphore_wait(barrier, fixed + jnp.where(at_home, 0, 2))

    def chunk(m):
        return pl.ds(m * JC, JC)

    started = []

    def start(copy):
        copy.start()
        started.append(copy)
        return copy

    twin_copies = [
        rcopy(g_all.at[r, chunk(m)], g_all.at[r, chunk(m)], TWIN + m, twin) for m in range(CHUNKS)
    ]
    start(twin_copies[0])
    a_copies = [
        rcopy(a_ref, a_all.at[place, r], A_ONE + d, out_a[d], A_ONE + r) for d in range(8)
    ]
    a_waits = [
        rcopy(a_ref, a_all.at[place, r], A_ONE + d, out_a[d], A_ONE + (r + d) % 8)
        for d in range(8)
    ]

    @pl.when(jnp.logical_not(at_home))
    def _():
        a_copies[0].start()

    for d in range(1, 8):
        start(a_copies[d])
    for m in range(1, CHUNKS):
        start(twin_copies[m])
    own_copies = [start(rcopy(g_all.at[r], g_all.at[r], Y_OWN + n, y_peers[n])) for n in range(3)]

    wt[96:128, :] = jnp.zeros((32, 4096), BF16)

    def prep_w(c, _):
        w = w_ref[pl.ds(pl.multiple_of(c * 32, 32), 32), :]
        lanes = pl.ds(pl.multiple_of(c * 128, 128), 128)
        h = w.astype(BF16)
        l = (w - h.astype(F32)).astype(BF16)
        wt[0:32, lanes] = h
        wt[32:64, lanes] = l
        wt[64:96, lanes] = h
        return 0

    lax.fori_loop(0, 32, prep_w, 0)

    for s in range(32):
        v = b_ref[:, s * 32 : (s + 1) * 32]
        h = high(v)
        bs[s * 32 : (s + 1) * 32, :] = jnp.concatenate([h, h, v - h, jnp.zeros_like(v)], axis=1)
    for j in range(32):
        v = bs[pl.ds(j, 32, stride=32), :]
        bjs[j * 32 : (j + 1) * 32, :] = v
        bp[j * 32 : (j + 1) * 32, :] = v.astype(BF16)
    for n in range(8):
        bt[:, n * 128 : (n + 1) * 128] = bjs[n * 128 : (n + 1) * 128, :].T.astype(BF16)

    def make_t(m):
        def step(cp, _):
            v = jnp.dot(
                bp[m * JC * 32 : (m + 1) * JC * 32, :],
                wt[:, pl.ds(pl.multiple_of(cp * 256, 256), 256)],
                preferred_element_type=F32,
            )
            h = v.astype(BF16)
            l = (v - h.astype(F32)).astype(BF16)
            for cc in range(2):
                rows = pl.ds(pl.multiple_of(cp * 64 + cc * 32, 32), 32)
                for j in range(JC):
                    lanes = slice((m * JC + j) * 128, (m * JC + j + 1) * 128)
                    t_h[rows, lanes] = h[j * 32 : (j + 1) * 32, cc * 128 : (cc + 1) * 128]
                    t_l[rows, lanes] = l[j * 32 : (j + 1) * 32, cc * 128 : (cc + 1) * 128]
            return 0

        lax.fori_loop(0, 16, step, 0)

    forwards = {}

    def forward(m):
        twin_copies[m].wait_recv()
        for n in range(3):
            src = g_all.at[r + 1 - 2 * zh, chunk(m)]
            forwards[m, n] = start(rcopy(src, src, FWD + 3 * m + n, y_peers[n]))

    make_t(0)
    make_t(1)
    for d in range(1, 8):
        a_waits[d].wait_recv()

    @pl.when(jnp.logical_not(at_home))
    def _():
        a_waits[0].wait_recv()

    ax_copies = [
        start(rcopy(a_all.at[place], a_all.at[place], A_X + n, x_peers[n])) for n in range(3)
    ]
    forward(0)
    make_t(2)
    for copy in ax_copies:
        copy.wait_recv()
    half = a_all.at[pl.ds(core * 4, 4)]
    ac_copy = start(rcopy(half, half, A_CORE, sibling))
    forward(1)
    make_t(3)
    ac_copy.wait_recv()
    zeros = jnp.zeros((64, 128), F32)
    for core_ in range(2):
        for x_ in range(4):
            v = a_all[core_ * 4 + x_].reshape(64, 128)
            h = high(v)
            rows = slice((x_ * 2 + core_) * 128, (x_ * 2 + core_ + 1) * 128)
            at1[rows, :] = jnp.concatenate([h, h], axis=0).T
            at2[rows, :] = jnp.concatenate([v - h, zeros], axis=0).T
    for c in range(32):
        ap[c * 32 : (c + 1) * 32, 0:128] = at1[pl.ds(c, 32, stride=32), :].astype(BF16)
        ap[c * 32 : (c + 1) * 32, 128:256] = at2[pl.ds(c, 32, stride=32), :].astype(BF16)
    gi[192:256, :] = jnp.zeros((64, JC * 128), BF16)
    for copy in own_copies:
        copy.wait_recv()

    rows_m = JC * 32
    for m in range(CHUNKS):
        for n in range(3):
            forwards[m, n].wait_recv()
        for j in range(JC):
            v = g_all[:, m * JC + j].reshape(64, 128)
            h = v.astype(BF16)
            l = (v - h.astype(F32)).astype(BF16)
            gi[0:64, j * 128 : (j + 1) * 128] = h
            gi[64:128, j * 128 : (j + 1) * 128] = l
            gi[128:192, j * 128 : (j + 1) * 128] = h

        def make_u(n, _):
            v_rows = pl.ds(pl.multiple_of(n * 256, 256), 256)
            for jp in range(JC // 2):
                v = jnp.dot(
                    ap[v_rows, :], gi[:, jp * 256 : (jp + 1) * 256], preferred_element_type=F32
                )
                h = v.astype(BF16)
                l = (v - h.astype(F32)).astype(BF16)
                for jj in range(2):
                    rows = slice((m * JC + jp * 2 + jj) * 32, (m * JC + jp * 2 + jj + 1) * 32)
                    for c in range(8):
                        lanes = pl.ds(pl.multiple_of(n * 1024 + c * 128, 128), 128)
                        u_h[rows, lanes] = h[c * 32 : (c + 1) * 32, jj * 128 : (jj + 1) * 128]
                        u_l[rows, lanes] = l[c * 32 : (c + 1) * 32, jj * 128 : (jj + 1) * 128]
            return 0

        lax.fori_loop(0, 4, make_u, 0)

        def add_w(cp, _):
            lanes = pl.ds(pl.multiple_of(cp * 256, 256), 256)
            left = bt[32:96, m * rows_m : (m + 1) * rows_m]
            v = jnp.dot(
                left, u_h[m * rows_m : (m + 1) * rows_m, lanes], preferred_element_type=F32
            ) + jnp.dot(left, u_l[m * rows_m : (m + 1) * rows_m, lanes], preferred_element_type=F32)
            acc_w[:, lanes] = v if m == 0 else acc_w[:, lanes] + v
            return 0

        lax.fori_loop(0, 16, add_w, 0)
        if m + 2 < CHUNKS:
            forward(m + 2)

        def add_a(n, _):
            rows = pl.ds(pl.multiple_of(n * 256, 256), 256)
            lanes = slice(m * JC * 128, (m + 1) * JC * 128)
            v = lax.dot_general(
                t_h[rows, lanes], gi[0:128, :], CONTRACT_LANES, preferred_element_type=F32
            ) + lax.dot_general(
                t_l[rows, lanes], gi[0:128, :], CONTRACT_LANES, preferred_element_type=F32
            )
            acc_a[rows, :] = v if m == 0 else acc_a[rows, :] + v
            return 0

        lax.fori_loop(0, 4, add_a, 0)

    def fold_w(c, _):
        lanes = pl.ds(pl.multiple_of(c * 128, 128), 128)
        gw_part[pl.ds(pl.multiple_of(c * 32, 32), 32), :] = (
            acc_w[0:32, lanes] + acc_w[32:64, lanes]
        ) * (1.0 / S)
        return 0

    lax.fori_loop(0, 32, fold_w, 0)
    other = pl.ds(pl.multiple_of((1 - core) * 512, 512), 512)
    w_core = start(rcopy(gw_part.at[other], gw_r1, W_CORE, sibling))
    b_core = start(rcopy(bias_own, bias_r1, B_CORE, sibling))

    for core_ in range(2):
        for x_ in range(4):
            s0 = 4 * (x_ * 2 + core_)
            v = jnp.concatenate(
                [acc_a[pl.ds(s0 + s, 32, stride=32), :] for s in range(4)], axis=0
            ).T
            ga_all[core_, x_] = ((v[0:64] + v[64:128]) * (1.0 / S)).reshape(8, 8, 128)
    ga_core = start(rcopy(ga_all.at[1 - core], ga_r1, GA_CORE, sibling))

    w_core.wait_recv()
    b_core.wait_recv()
    bias = bias_own[...] + bias_r1[...]

    def add_core(n, _):
        rows = pl.ds(pl.multiple_of(n * 32, 32), 32)
        mine = pl.ds(pl.multiple_of(core * 512 + n * 32, 32), 32)
        gw_s[n, 0:32] = gw_part[mine, :] + gw_r1[rows, :]
        gw_s[n, 32:40] = bias
        return 0

    lax.fori_loop(0, 16, add_core, 0)
    gw_r2[xy] = gw_s[xy]
    w_xy = []
    for n, (dx, dy) in enumerate(xy_steps):
        to = ((x + dx) % 4) * 4 + (y + dy) % 4
        w_xy.append(start(rcopy(gw_s.at[to], gw_r2.at[xy], W_XY + n, xy_peers[n])))

    ga_core.wait_recv()
    for x_ in range(4):
        ga_r1[x_] = ga_r1[x_] + ga_all[core, x_]
    ga_r2[x] = ga_r1[x]
    ga_x = []
    for n, d in enumerate((1, 2, 3)):
        ga_x.append(start(rcopy(ga_r1.at[(x + d) % 4], ga_r2.at[x], GA_X + n, x_peers[n])))

    def add_b(m):
        rows = slice(m * rows_m, (m + 1) * rows_m)

        def step(n, v):
            lanes = pl.ds(pl.multiple_of(n * 1024, 1024), 1024)
            right = wt[0:64, lanes]
            return (
                v
                + lax.dot_general(u_h[rows, lanes], right, CONTRACT_LANES, preferred_element_type=F32)
                + lax.dot_general(u_l[rows, lanes], right, CONTRACT_LANES, preferred_element_type=F32)
            )

        v = lax.fori_loop(0, 4, step, jnp.zeros((rows_m, 64), F32))
        bjs[rows, 0:32] = (v[:, 0:32] + v[:, 32:64]) * (1.0 / S)

    add_b(0)
    for copy in w_xy:
        copy.wait_recv()
    v = gw_r2[0]
    for n in range(1, 16):
        v = v + gw_r2[n]
    gw_z1[z % 4] = v
    w_z1 = [
        start(rcopy(gw_z1.at[z % 4], gw_z1.at[z % 4], W_Z1 + n, z_near[n])) for n in range(3)
    ]
    for copy in ga_x:
        copy.wait_recv()
    ga_s[...] = (ga_r2[0] + ga_r2[1]) + (ga_r2[2] + ga_r2[3])
    ga_z = [
        rcopy(ga_s.at[(r + d) % 8], ga_r3.at[zl], GA_Z + d, in_a[d], GA_Z + zl) for d in range(8)
    ]
    ga_waits = [
        rcopy(ga_s.at[d], ga_r3.at[zl], GA_Z + d, in_a[d], GA_Z + (zl + d) % 8) for d in range(8)
    ]

    @pl.when(jnp.logical_not(at_home))
    def _():
        ga_z[0].start()

    @pl.when(at_home)
    def _():
        ga_r3[zl] = ga_s[r]

    for d in range(1, 8):
        start(ga_z[d])
    add_b(1)
    for copy in w_z1:
        copy.wait_recv()
    gw_z2[z // 4] = (gw_z1[0] + gw_z1[1]) + (gw_z1[2] + gw_z1[3])
    w_z2 = [
        start(rcopy(gw_z2.at[z // 4], gw_z2.at[z // 4], W_Z2 + n, z_far[n])) for n in range(3)
    ]
    add_b(2)
    add_b(3)
    for s in range(32):
        gb_out[:, s * 32 : (s + 1) * 32] = bjs[pl.ds(s, 32, stride=32), 0:32]
    for copy in w_z2:
        copy.wait_recv()
    v = (gw_z2[0] + gw_z2[1]) + (gw_z2[2] + gw_z2[3])
    mine = pl.ds(pl.multiple_of(core * 512 + xy * 32, 32), 32)
    gw_out[mine, :] = v[0:32]
    bias_out[...] = jnp.sum(v[32:40], axis=0, keepdims=True)
    w_ag = [
        start(rcopy(gw_out.at[mine], gw_out.at[mine], W_AG + n, xy_peers[n])) for n in range(15)
    ]
    for d in range(1, 8):
        ga_waits[d].wait_recv()

    @pl.when(jnp.logical_not(at_home))
    def _():
        ga_waits[0].wait_recv()

    v = ga_r3[0]
    for n in range(1, 8):
        v = v + ga_r3[n]
    ga_out[...] = v
    for copy in w_ag:
        copy.wait_recv()
    mine = gw_out.at[pl.ds(pl.multiple_of(core * 512, 512), 512)]
    w_end = start(rcopy(mine, mine, W_END, sibling))
    w_end.wait_recv()
    for copy in started:
        copy.wait_send()

    @pl.when(jnp.logical_not(at_home))
    def _():
        a_copies[0].wait_send()
        ga_z[0].wait_send()


def local(side_a, side_b, pair_grad, out_weight):
    vmem = pl.BlockSpec(memory_space=pltpu.VMEM)
    flat = pair_grad.reshape(256, K)
    ga, gb, gw, bias = pl.pallas_call(
        kernel,
        out_shape=(
            jax.ShapeDtypeStruct((8, 128), F32),
            jax.ShapeDtypeStruct((32, 1024), F32),
            jax.ShapeDtypeStruct((1024, 128), F32),
            jax.ShapeDtypeStruct((1, 128), F32),
        ),
        in_specs=[vmem] * 4,
        out_specs=(vmem,) * 4,
        scratch_shapes=[
            pltpu.VMEM((8, 32, 8, 128), F32),
            pltpu.VMEM((8, 8, 8, 128), F32),
            pltpu.VMEM((2, 4, 8, 8, 128), F32),
            pltpu.VMEM((4, 8, 8, 128), F32),
            pltpu.VMEM((4, 8, 8, 128), F32),
            pltpu.VMEM((8, 8, 128), F32),
            pltpu.VMEM((8, 8, 128), F32),
            pltpu.VMEM((1024, 128), F32),
            pltpu.VMEM((512, 128), F32),
            pltpu.VMEM((16, 40, 128), F32),
            pltpu.VMEM((16, 40, 128), F32),
            pltpu.VMEM((4, 40, 128), F32),
            pltpu.VMEM((4, 40, 128), F32),
            pltpu.VMEM((8, 128), F32),
            pltpu.VMEM((8, 128), F32),
            pltpu.VMEM((1024, 4096), BF16),
            pltpu.VMEM((1024, 4096), BF16),
            pltpu.VMEM((1024, 4096), BF16),
            pltpu.VMEM((1024, 4096), BF16),
            pltpu.VMEM((128, 4096), BF16),
            pltpu.VMEM((1024, 128), F32),
            pltpu.VMEM((1024, 128), F32),
            pltpu.VMEM((1024, 128), BF16),
            pltpu.VMEM((128, 1024), BF16),
            pltpu.VMEM((1024, 128), F32),
            pltpu.VMEM((1024, 128), F32),
            pltpu.VMEM((1024, 256), BF16),
            pltpu.VMEM((256, JC * 128), BF16),
            pltpu.VMEM((1024, 128), F32),
            pltpu.VMEM((64, 4096), F32),
            pltpu.SemaphoreType.DMA((N_SEM,)),
            pltpu.SemaphoreType.DMA((N_SEM,)),
        ],
        compiler_params=pltpu.CompilerParams(
            collective_id=0, has_side_effects=True, vmem_limit_bytes=60 * 1024 * 1024
        ),
    )(side_a, side_b, flat, out_weight)
    return ga, gb, gw, bias.reshape(K)


def solution(mesh):
    in_specs = (P("row", "col"), P("col", "row"), P("row", "col", None), P())
    out_specs = (P("row", "col"), P("col", "row"), P(), P())
    return jax.shard_map(local, mesh=mesh, in_specs=in_specs, out_specs=out_specs, check_vma=False)
```

time: 1650 us -> 104 us (0.06)
  waiting for transfers between devices: 1310 us -> 0 us
  blocking collectives: 279 us -> 0 us
  Pallas kernels: 0 us -> 98.3 us
  local copies, waits for them, and re-layouts: 37.5 us -> 5.22 us
    psum x3 -> x0, waiting for transfers between devices: 1300 us -> none  [the longest x1 783 us: local(): left_total = lax.psum(left_part, 'col')]
    psum x1 -> x0, blocking collectives: 149 us -> none  [local(): weight_sums = lax.psum((weight_part, bias_part), ('row', 'col'))]
    all_gather x1 -> x0, blocking collectives: 130 us -> none  [local(): left = lax.all_gather(side_a, 'col', axis=1, tiled=True).reshape(rows, S, C)]
    pallas_call x0 -> x1, Pallas kernels: none -> 98.3 us  [local(): pl.pallas_call(kernel, out_shape=(jax.ShapeDtypeStruct((8, 128), F32), ja...]
    reshape x10 -> x0, local copies, waits for them, and re-layouts: 29.4 us -> none  [the longest x2 9.24 us: local(): outer.reshape(rows, C, cols, C)]
  transfers between devices with their start and end apart: 4 -> 0, of which waited for: 3 -> 0; matrix products, arithmetic and copies ran while one was open for 3% -> 0% of each run, Pallas kernels for 0% -> 0%
where the time goes in v1:
time: 104 us
  Pallas kernels  98.3 us (95%)
  local copies, waits for them, and re-layouts  5.22 us (5%)
    pallas_call x1, Pallas kernels, local(): pl.pallas_call(kernel, out_shape=(jax.ShapeDtypeStruct((8, 128), F32), ja...  98.3 us
    unnamed x8, local copies, waits for them, and re-layouts  5.22 us

profile of v1, /device:TPU:1, one launch (start us, length us, event | category | flops | bytes accessed | tf_op | source)
XLA Modules:
  0.0 104.2 jit_solution(2329395199427713553)
XLA Ops:
  0.6 98.3 %shard_map.75 = (f32[8,128]{1,0:T(8,128)}, f32[32,1024]{1,0:T(8,128)}, f32[1024,128]{1,0:T(8,128)}, f32[1,128]{1,0:T(1,128)}) custom-call(f32[8,128]{1,0:T(8,128)} %a_ref.1, f32[32,1024]{1,0:T(8,128)} %b_ref.1, f32[256,128]{1,0:T(8,128)} %bitcast.2, f32[1024,128]{1,0:T(8,128)} %w_ref.1), custom_call_target="tpu_custom_call" | custom-call | tf_op jit(solution)/shard_map/pallas_call | solution.py:463
  99.0 0.0 copy-start
  99.0 0.7 copy-done
  99.7 0.6 copy.12
  100.3 1.6 %copy.13 = f32[32,1024]{1,0:T(8,128)} copy(f32[32,1024]{1,0:T(8,128)} %get-tuple-element.17) | data formatting | bytes 262144
  101.8 0.0 copy-start.1
  101.8 1.9 %copy.14 = f32[1024,128]{1,0:T(8,128)} copy(f32[1024,128]{1,0:T(8,128)} %get-tuple-element.18) | data formatting | bytes 1048576
  103.7 0.0 copy-done.1
  103.7 0.5 copy.15
Async XLA Ops:
  99.0 0.7 copy-start
  101.8 1.9 %copy-start.1 = (f32[1,128]{1,0:T(1,128)S(1)}, f32[1,128]{1,0:T(1,128)}, u32[]{:S(2)}) copy-start(f32[1,128]{1,0:T(1,128)} %get-tuple-element.11) | copy-start | bytes 1540

commit v2 on v1

v2 whole, which is shorter than its diff:
```python
import jax
import jax.numpy as jnp
from jax import lax
from jax.experimental import pallas as pl
from jax.experimental.pallas import tpu as pltpu
from jax.sharding import PartitionSpec as P

S = 256
C = 32
K = 128
CHUNKS = 8
TC = 32 // CHUNKS
JC = 8
MESH = pl.DeviceIdType.MESH
F32 = jnp.float32
BF16 = jnp.bfloat16

Y_OWN = 0
TWIN = Y_OWN + 3
FWD = TWIN + CHUNKS
A_ONE = FWD + 3 * CHUNKS
A_X = A_ONE + 8
A_CORE = A_X + 3
GA_CORE = A_CORE + 1
GA_X = GA_CORE + 1
GA_Z = GA_X + 3
W_CORE = GA_Z + 8
B_CORE = W_CORE + 1
W_XY = B_CORE + 1
W_Z1 = W_XY + 16
W_Z2 = W_Z1 + 3
W_AG = W_Z2 + 3
W_END = W_AG + 16
N_SEM = W_END + 1

CONTRACT_LANES = (((1,), (1,)), ((), ()))


def high(x):
    return x.astype(BF16).astype(F32)


def kernel(
    a_ref,
    b_ref,
    pg_ref,
    w_ref,
    ga_out,
    gb_out,
    gw_out,
    bias_out,
    g_all,
    a_all,
    ga_all,
    ga_r1,
    ga_r2,
    ga_s,
    ga_r3,
    gw_part,
    gw_r1,
    gw_s,
    gw_r2,
    gw_z1,
    gw_z2,
    bias_own,
    bias_r1,
    o_h,
    o_l,
    d_h,
    d_l,
    wp,
    bs,
    bo,
    bg,
    at,
    az,
    gp,
    acc_a,
    acc_w,
    bjs,
    send_sem,
    recv_sem,
):
    r = lax.axis_index("row")
    q = lax.axis_index("col")
    y = r // 2
    zh = r % 2
    zl = q // 8
    x = (q // 2) % 4
    core = q % 2
    z = zh * 8 + zl
    place = core * 4 + x
    xy = x * 4 + y

    def dev(y_, z_, x_, core_):
        return (y_ * 2 + z_ // 8, (z_ % 8) * 8 + x_ * 2 + core_)

    def rcopy(src, dst, number, device, arrives=None):
        return pltpu.make_async_remote_copy(
            src_ref=src,
            dst_ref=dst,
            send_sem=send_sem.at[number],
            recv_sem=recv_sem.at[number if arrives is None else arrives],
            device_id=device,
            device_id_type=MESH,
        )

    sibling = dev(y, z, x, 1 - core)
    twin = dev(y, (z + 8) % 16, x, core)
    y_peers = [dev((y + d) % 4, z, x, core) for d in (1, 2, 3)]
    x_peers = [dev(y, z, (x + d) % 4, core) for d in (1, 2, 3)]
    xy_steps = [(dx, dy) for dx in range(4) for dy in range(4) if (dx, dy) != (0, 0)]
    xy_peers = [dev((y + dy) % 4, z, (x + dx) % 4, core) for dx, dy in xy_steps]
    z_near = [dev(y, (z // 4) * 4 + (z + d) % 4, x, core) for d in (1, 2, 3)]
    z_far = [dev(y, (z + 4 * d) % 16, x, core) for d in (1, 2, 3)]
    out_a = [(zl, ((zl + d) % 8) * 8 + x * 2 + core) for d in range(8)]
    in_a = [((r + d) % 8, r * 8 + x * 2 + core) for d in range(8)]
    at_home = zl == r

    barrier = pltpu.get_barrier_semaphore()

    def greet(device):
        pl.semaphore_signal(barrier, inc=1, device_id=device, device_id_type=MESH)

    for device in out_a[1:] + in_a[1:] + z_far + z_near + xy_peers + [sibling]:
        greet(device)

    @pl.when(jnp.logical_not(at_home))
    def _():
        greet(out_a[0])
        greet(in_a[0])

    bias = jnp.zeros((8, K), F32)
    for j in range(32):
        block = pg_ref[pl.ds(j, 8, stride=32), :]
        g_all[r, j] = block
        bias = bias + block
    bias_own[...] = bias

    @pl.when(at_home)
    def _():
        a_all[place, r] = a_ref[...]

    fixed = 14 + 3 + 3 + 15 + 1
    pl.semaphore_wait(barrier, fixed + jnp.where(at_home, 0, 2))

    def chunk(m):
        return pl.ds(m * TC, TC)

    started = []

    def start(copy):
        copy.start()
        started.append(copy)
        return copy

    twin_copies = [
        rcopy(g_all.at[r, chunk(m)], g_all.at[r, chunk(m)], TWIN + m, twin) for m in range(CHUNKS)
    ]
    a_copies = [
        rcopy(a_ref, a_all.at[place, r], A_ONE + d, out_a[d], A_ONE + r) for d in range(8)
    ]
    a_waits = [
        rcopy(a_ref, a_all.at[place, r], A_ONE + d, out_a[d], A_ONE + (r + d) % 8)
        for d in range(8)
    ]

    @pl.when(jnp.logical_not(at_home))
    def _():
        a_copies[0].start()

    for d in range(1, 8):
        start(a_copies[d])
    for m in range(CHUNKS):
        start(twin_copies[m])
    own_copies = [start(rcopy(g_all.at[r], g_all.at[r], Y_OWN + n, y_peers[n])) for n in range(3)]

    low_lanes = lax.broadcasted_iota(jnp.int32, (32, 128), 1) < 64

    def split(v):
        h = v.astype(BF16)
        return h, (v - h.astype(F32)).astype(BF16)

    def prep_w(n, _):
        rows = pl.ds(pl.multiple_of(n * 128, 128), 128)
        h, l = split(w_ref[rows, :])
        wp[rows, 0:128] = h
        wp[rows, 128:256] = l
        wp[rows, 256:384] = h
        return 0

    lax.fori_loop(0, 8, prep_w, 0)

    for s in range(32):
        bs[s * 32 : (s + 1) * 32, 0:32] = b_ref[:, s * 32 : (s + 1) * 32]
    for jq in range(4):
        lanes = slice(jq * 128, (jq + 1) * 128)
        parts = []
        for jj in range(2):
            v = jnp.concatenate(
                [bs[pl.ds(8 * jq + 2 * t + jj, 32, stride=32), :][:, 0:32] for t in range(4)],
                axis=1,
            )
            h = high(v)
            parts.append((h, v - h))
            bg[jj * 32 : (jj + 1) * 32, lanes] = h.astype(BF16)
            bg[64 + jj * 32 : 64 + (jj + 1) * 32, lanes] = (v - h).astype(BF16)
        for n in range(2):
            v = jnp.concatenate([parts[0][n], parts[1][n]] * 2, axis=0)
            bo[lanes, n * 128 : (n + 1) * 128] = v.T.astype(BF16)

    forwards = {}

    def forward(m):
        twin_copies[m].wait_recv()
        for n in range(3):
            src = g_all.at[r + 1 - 2 * zh, chunk(m)]
            forwards[m, n] = start(rcopy(src, src, FWD + 3 * m + n, y_peers[n]))

    def prep_g(m):
        for n in range(3):
            forwards[2 * m, n].wait_recv()
            forwards[2 * m + 1, n].wait_recv()
        for j in range(m * JC, (m + 1) * JC):
            rows = slice(j * 64, (j + 1) * 64)
            gp[rows, 0:128], gp[rows, 128:256] = split(g_all[:, j].reshape(64, 128))

    def grad_outer(m):
        right = slice(m * JC * 64, (m + 1) * JC * 64)

        def make_d(n, _):
            for c2 in range(2):
                rows = pl.ds(pl.multiple_of(n * 256 + c2 * 128, 128), 128)
                v = lax.dot_general(
                    wp[rows, 0:256], gp[right, :], CONTRACT_LANES, preferred_element_type=F32
                ) + lax.dot_general(
                    wp[rows, 128:384], gp[right, :], CONTRACT_LANES, preferred_element_type=F32
                )
                h, l = split(v)
                for c in range(4):
                    lanes = pl.ds(pl.multiple_of(n * 1024 + (c2 * 4 + c) * 128, 128), 128)
                    for jp in range(4):
                        rows = slice((m * 4 + jp) * 32, (m * 4 + jp + 1) * 32)
                        part = (slice(c * 32, (c + 1) * 32), slice(jp * 128, (jp + 1) * 128))
                        d_h[rows, lanes] = h[part]
                        d_l[rows, lanes] = l[part]
            return 0

        lax.fori_loop(0, 4, make_d, 0)

    forward(0)
    for d in range(1, 8):
        a_waits[d].wait_recv()

    @pl.when(jnp.logical_not(at_home))
    def _():
        a_waits[0].wait_recv()

    ax_copies = [
        start(rcopy(a_all.at[place], a_all.at[place], A_X + n, x_peers[n])) for n in range(3)
    ]
    for m in range(1, 4):
        forward(m)
    for copy in ax_copies:
        copy.wait_recv()
    half = a_all.at[pl.ds(core * 4, 4)]
    ac_copy = start(rcopy(half, half, A_CORE, sibling))
    forward(4)
    for copy in own_copies:
        copy.wait_recv()
    prep_g(0)
    ac_copy.wait_recv()
    for core_ in range(2):
        for x_ in range(4):
            v = a_all[core_ * 4 + x_].reshape(64, 128)
            rows = slice((x_ * 2 + core_) * 128, (x_ * 2 + core_ + 1) * 128)
            at[rows, :] = jnp.concatenate([v, v], axis=0).T
    for c in range(32):
        v = at[pl.ds(c, 32, stride=32), :]
        h = high(v)
        l = v - h
        zero = jnp.zeros_like(v)
        v = jnp.concatenate(
            [
                jnp.where(low_lanes, h, zero),
                jnp.where(low_lanes, zero, h),
                jnp.where(low_lanes, l, zero),
                jnp.where(low_lanes, zero, l),
            ],
            axis=0,
        ).astype(BF16)
        lanes = slice(c * 128, (c + 1) * 128)
        az[0:128, lanes] = v
        az[128:256, lanes] = v
    forward(5)

    def make_o(n, _):
        right = az[:, pl.ds(pl.multiple_of(n * 256, 256), 256)]
        for jq in range(4):
            v = jnp.dot(bo[jq * 128 : (jq + 1) * 128, :], right, preferred_element_type=F32)
            h, l = split(v)
            for t in range(4):
                lanes = slice((jq * 4 + t) * 128, (jq * 4 + t + 1) * 128)
                for cc in range(2):
                    rows = pl.ds(pl.multiple_of(n * 64 + cc * 32, 32), 32)
                    part = (slice(t * 32, (t + 1) * 32), slice(cc * 128, (cc + 1) * 128))
                    o_h[rows, lanes] = h[part]
                    o_l[rows, lanes] = l[part]
        return 0

    lax.fori_loop(0, 8, make_o, 0)
    forward(6)
    lax.fori_loop(8, 16, make_o, 0)
    forward(7)

    for m in range(4):
        if m:
            prep_g(m)

        def add_w(n, _):
            rows = pl.ds(pl.multiple_of(n * 256, 256), 256)
            lanes = slice(m * 512, (m + 1) * 512)
            right = gp[m * 512 : (m + 1) * 512, :]
            v = jnp.dot(o_h[rows, lanes], right, preferred_element_type=F32) + jnp.dot(
                o_l[rows, lanes], right, preferred_element_type=F32
            )
            if m:
                v = v + acc_w[rows, :]
            if m < 3:
                acc_w[rows, :] = v
            else:
                gw_part[rows, :] = (v[:, 0:128] + v[:, 128:256]) * (1.0 / S)
            return 0

        lax.fori_loop(0, 4, add_w, 0)

    other = pl.ds(pl.multiple_of((1 - core) * 512, 512), 512)
    w_core = start(rcopy(gw_part.at[other], gw_r1, W_CORE, sibling))
    b_core = start(rcopy(bias_own, bias_r1, B_CORE, sibling))

    grad_outer(0)
    w_core.wait_recv()
    b_core.wait_recv()
    bias = bias_own[...] + bias_r1[...]

    def add_core(n, _):
        rows = pl.ds(pl.multiple_of(n * 32, 32), 32)
        mine = pl.ds(pl.multiple_of(core * 512 + n * 32, 32), 32)
        gw_s[n, 0:32] = gw_part[mine, :] + gw_r1[rows, :]
        gw_s[n, 32:40] = bias
        return 0

    lax.fori_loop(0, 16, add_core, 0)
    gw_r2[xy] = gw_s[xy]
    w_xy = []
    for n, (dx, dy) in enumerate(xy_steps):
        to = ((x + dx) % 4) * 4 + (y + dy) % 4
        w_xy.append(start(rcopy(gw_s.at[to], gw_r2.at[xy], W_XY + n, xy_peers[n])))

    def add_b(m):
        rows = slice(m * 128, (m + 1) * 128)
        v = jnp.zeros((128, 128), F32)
        for n in range(4):
            lanes = slice(n * 1024, (n + 1) * 1024)
            v = v + lax.dot_general(
                d_h[rows, lanes], az[0:128, lanes], CONTRACT_LANES, preferred_element_type=F32
            )
            v = v + lax.dot_general(
                d_l[rows, lanes], az[0:128, lanes], CONTRACT_LANES, preferred_element_type=F32
            )
        v = v.T
        v = (v[0:64] + v[64:128]) * (1.0 / S)
        for t in range(4):
            jp = m * 4 + t
            bjs[jp * 64 : (jp + 1) * 64, 0:32] = v[:, t * 32 : (t + 1) * 32]

    for m in range(1, 4):
        grad_outer(m)
    for copy in w_xy:
        copy.wait_recv()
    v = gw_r2[0]
    for n in range(1, 16):
        v = v + gw_r2[n]
    gw_z1[z % 4] = v
    w_z1 = [
        start(rcopy(gw_z1.at[z % 4], gw_z1.at[z % 4], W_Z1 + n, z_near[n])) for n in range(3)
    ]
    def add_a(n, _):
        lanes = pl.ds(pl.multiple_of(n * 256, 256), 256)
        v = jnp.dot(bg[...], d_h[:, lanes], preferred_element_type=F32) + jnp.dot(
            bg[...], d_l[:, lanes], preferred_element_type=F32
        )
        v = v[0:64] + v[64:128]
        for cc in range(2):
            part = v[:, cc * 128 : (cc + 1) * 128]
            rows = pl.ds(pl.multiple_of(n * 64 + cc * 32, 32), 32)
            acc_a[rows, :] = jnp.where(low_lanes, part[0:32], part[32:64])
        return 0

    lax.fori_loop(0, 16, add_a, 0)
    for core_ in range(2):
        for x_ in range(4):
            s0 = 4 * (x_ * 2 + core_)
            v = jnp.concatenate(
                [acc_a[pl.ds(s0 + s, 32, stride=32), :] for s in range(4)], axis=0
            ).T
            ga_all[core_, x_] = ((v[0:64] + v[64:128]) * (1.0 / S)).reshape(8, 8, 128)
    ga_core = start(rcopy(ga_all.at[1 - core], ga_r1, GA_CORE, sibling))

    for copy in w_z1:
        copy.wait_recv()
    gw_z2[z // 4] = (gw_z1[0] + gw_z1[1]) + (gw_z1[2] + gw_z1[3])
    w_z2 = [
        start(rcopy(gw_z2.at[z // 4], gw_z2.at[z // 4], W_Z2 + n, z_far[n])) for n in range(3)
    ]
    ga_core.wait_recv()
    for x_ in range(4):
        ga_r1[x_] = ga_r1[x_] + ga_all[core, x_]
    ga_r2[x] = ga_r1[x]
    ga_x = []
    for n, d in enumerate((1, 2, 3)):
        ga_x.append(start(rcopy(ga_r1.at[(x + d) % 4], ga_r2.at[x], GA_X + n, x_peers[n])))

    add_b(0)
    add_b(1)
    for copy in ga_x:
        copy.wait_recv()
    ga_s[...] = (ga_r2[0] + ga_r2[1]) + (ga_r2[2] + ga_r2[3])
    ga_z = [
        rcopy(ga_s.at[(r + d) % 8], ga_r3.at[zl], GA_Z + d, in_a[d], GA_Z + zl) for d in range(8)
    ]
    ga_waits = [
        rcopy(ga_s.at[d], ga_r3.at[zl], GA_Z + d, in_a[d], GA_Z + (zl + d) % 8) for d in range(8)
    ]

    @pl.when(jnp.logical_not(at_home))
    def _():
        ga_z[0].start()

    @pl.when(at_home)
    def _():
        ga_r3[zl] = ga_s[r]

    for d in range(1, 8):
        start(ga_z[d])
    for copy in w_z2:
        copy.wait_recv()
    v = (gw_z2[0] + gw_z2[1]) + (gw_z2[2] + gw_z2[3])
    mine = pl.ds(pl.multiple_of(core * 512 + xy * 32, 32), 32)
    gw_out[mine, :] = v[0:32]
    w_ag = [
        start(rcopy(gw_out.at[mine], gw_out.at[mine], W_AG + n, xy_peers[n])) for n in range(15)
    ]
    bias_out[...] = jnp.sum(v[32:40], axis=0, keepdims=True)
    add_b(2)
    add_b(3)
    for s in range(32):
        gb_out[:, s * 32 : (s + 1) * 32] = bjs[pl.ds(s, 32, stride=32), :][:, 0:32]
    for copy in w_ag:
        copy.wait_recv()
    mine = gw_out.at[pl.ds(pl.multiple_of(core * 512, 512), 512)]
    w_end = start(rcopy(mine, mine, W_END, sibling))
    for d in range(1, 8):
        ga_waits[d].wait_recv()

    @pl.when(jnp.logical_not(at_home))
    def _():
        ga_waits[0].wait_recv()

    v = ga_r3[0]
    for n in range(1, 8):
        v = v + ga_r3[n]
    ga_out[...] = v
    w_end.wait_recv()
    for copy in started:
        copy.wait_send()

    @pl.when(jnp.logical_not(at_home))
    def _():
        a_copies[0].wait_send()
        ga_z[0].wait_send()


def hand_over(*refs):
    for n in range(4):
        refs[4 + n][...] = refs[n][...]


def local(side_a, side_b, pair_grad, out_weight):
    vmem = pl.BlockSpec(memory_space=pltpu.VMEM)
    flat = pair_grad.reshape(256, K)
    ga, gb, gw, bias = pl.pallas_call(
        kernel,
        out_shape=(
            jax.ShapeDtypeStruct((8, 128), F32),
            jax.ShapeDtypeStruct((32, 1024), F32),
            jax.ShapeDtypeStruct((1024, 128), F32),
            jax.ShapeDtypeStruct((1, 128), F32),
        ),
        in_specs=[vmem] * 4,
        out_specs=(vmem,) * 4,
        scratch_shapes=[
            pltpu.VMEM((8, 32, 8, 128), F32),
            pltpu.VMEM((8, 8, 8, 128), F32),
            pltpu.VMEM((2, 4, 8, 8, 128), F32),
            pltpu.VMEM((4, 8, 8, 128), F32),
            pltpu.VMEM((4, 8, 8, 128), F32),
            pltpu.VMEM((8, 8, 128), F32),
            pltpu.VMEM((8, 8, 128), F32),
            pltpu.VMEM((1024, 128), F32),
            pltpu.VMEM((512, 128), F32),
            pltpu.VMEM((16, 40, 128), F32),
            pltpu.VMEM((16, 40, 128), F32),
            pltpu.VMEM((4, 40, 128), F32),
            pltpu.VMEM((4, 40, 128), F32),
            pltpu.VMEM((8, 128), F32),
            pltpu.VMEM((8, 128), F32),
            pltpu.VMEM((1024, 2048), BF16),
            pltpu.VMEM((1024, 2048), BF16),
            pltpu.VMEM((512, 4096), BF16),
            pltpu.VMEM((512, 4096), BF16),
            pltpu.VMEM((1024, 384), BF16),
            pltpu.VMEM((1024, 128), F32),
            pltpu.VMEM((512, 256), BF16),
            pltpu.VMEM((128, 512), BF16),
            pltpu.VMEM((1024, 128), F32),
            pltpu.VMEM((256, 4096), BF16),
            pltpu.VMEM((2048, 256), BF16),
            pltpu.VMEM((1024, 128), F32),
            pltpu.VMEM((1024, 256), F32),
            pltpu.VMEM((1024, 128), F32),
            pltpu.SemaphoreType.DMA((N_SEM,)),
            pltpu.SemaphoreType.DMA((N_SEM,)),
        ],
        compiler_params=pltpu.CompilerParams(
            collective_id=0, has_side_effects=True, vmem_limit_bytes=60 * 1024 * 1024
        ),
    )(side_a, side_b, flat, out_weight)
    arrays = (ga, gb, gw, bias)
    ga, gb, gw, bias = pl.pallas_call(
        hand_over,
        out_shape=tuple(jax.ShapeDtypeStruct(v.shape, v.dtype) for v in arrays),
        in_specs=[vmem] * 4,
        out_specs=(vmem,) * 4,
    )(*arrays)
    return ga, gb, gw, bias.reshape(K)


def solution(mesh):
    in_specs = (P("row", "col"), P("col", "row"), P("row", "col", None), P())
    out_specs = (P("row", "col"), P("col", "row"), P(), P())
    return jax.shard_map(local, mesh=mesh, in_specs=in_specs, out_specs=out_specs, check_vma=False)
```

time: 104 us -> 83.8 us (0.81)
  Pallas kernels: 98.3 us -> 82.7 us
  local copies, waits for them, and re-layouts: 5.22 us -> 0 us
    pallas_call x1, Pallas kernels: 98.3 us -> 80.8 us  [local(): pl.pallas_call(kernel, out_shape=(jax.ShapeDtypeStruct((8, 128), F32), ja...]
    unnamed x8 -> x0, local copies, waits for them, and re-layouts: 5.22 us -> none
    pallas_call x0 -> x1, Pallas kernels: none -> 1.98 us  [local(): pl.pallas_call(hand_over, out_shape=tuple((jax.ShapeDtypeStruct(v.shape,...]
where the time goes in v2:
time: 83.8 us; the launch traced here: 83.4 us
  Pallas kernels  82.7 us (99%)
    pallas_call x1, Pallas kernels, local(): pl.pallas_call(kernel, out_shape=(jax.ShapeDtypeStruct((8, 128), F32), ja...  80.8 us
    pallas_call x1, Pallas kernels, local(): pl.pallas_call(hand_over, out_shape=tuple((jax.ShapeDtypeStruct(v.shape,...  1.98 us

profile of v2, /device:TPU:1, one launch (start us, length us, event | category | flops | bytes accessed | tf_op | source)
XLA Modules:
  0.0 83.4 jit_solution(2656151231203614440)
XLA Ops:
  0.6 80.8 %shard_map.75 = (f32[8,128]{1,0:T(8,128)}, f32[32,1024]{1,0:T(8,128)}, f32[1024,128]{1,0:T(8,128)}, f32[1,128]{1,0:T(1,128)}) custom-call(f32[8,128]{1,0:T(8,128)} %a_ref.1, f32[32,1024]{1,0:T(8,128)} %b_ref.1, f32[256,128]{1,0:T(8,128)} %bitcast.2, f32[1024,128]{1,0:T(8,128)} %w_ref.1), custom_call_target="tpu_custom_call" | custom-call | tf_op jit(solution)/shard_map/pallas_call | solution.py:492
  81.4 2.0 %shard_map.76 = (f32[8,128]{1,0:T(8,128)}, f32[32,1024]{1,0:T(8,128)}, f32[1024,128]{1,0:T(8,128)}, f32[1,128]{1,0:T(1,128)}) custom-call(f32[8,128]{1,0:T(8,128)} %get-tuple-element.12.refs_0_, f32[32,1024]{1,0:T(8,128)} %get-tuple-element.13.refs_1_, f32[1024,128]{1,0:T(8,128)} %get-tuple-element.14.refs_2_, f32[1,128]{1,0:T(1,128)} %get-tuple-element.15.refs_3_), custom_call_target="tpu_custom_call" | custom-call | tf_op jit(solution)/shard_map/pallas_call | solution.py:540

commit v3 on v2

--- a/solution.py
+++ b/solution.py
@@ -31,7 +31,7 @@
 W_Z2 = W_Z1 + 3
 W_AG = W_Z2 + 3
 W_END = W_AG + 16
-N_SEM = W_END + 1
+N_SEM = W_END + 16
 
 CONTRACT_LANES = (((1,), (1,)), ((), ()))
 
@@ -75,6 +75,7 @@
     at,
     az,
     gp,
+    gt,
     acc_a,
     acc_w,
     bjs,
@@ -109,10 +110,11 @@
     twin = dev(y, (z + 8) % 16, x, core)
     y_peers = [dev((y + d) % 4, z, x, core) for d in (1, 2, 3)]
     x_peers = [dev(y, z, (x + d) % 4, core) for d in (1, 2, 3)]
-    xy_steps = [(dx, dy) for dx in range(4) for dy in range(4) if (dx, dy) != (0, 0)]
+    xy_steps = [(dx, dy) for dx in (2, 1, 3, 0) for dy in (2, 1, 3, 0) if (dx, dy) != (0, 0)]
+    xy_steps.sort(key=lambda step: sum(min(d, 4 - d) for d in step), reverse=True)
     xy_peers = [dev((y + dy) % 4, z, (x + dx) % 4, core) for dx, dy in xy_steps]
     z_near = [dev(y, (z // 4) * 4 + (z + d) % 4, x, core) for d in (1, 2, 3)]
-    z_far = [dev(y, (z + 4 * d) % 16, x, core) for d in (1, 2, 3)]
+    z_far = [dev(y, (z + 4 * d) % 16, x, core) for d in (2, 1, 3)]
     out_a = [(zl, ((zl + d) % 8) * 8 + x * 2 + core) for d in range(8)]
     in_a = [((r + d) % 8, r * 8 + x * 2 + core) for d in range(8)]
     at_home = zl == r
@@ -221,9 +223,13 @@
         for n in range(3):
             forwards[2 * m, n].wait_recv()
             forwards[2 * m + 1, n].wait_recv()
-        for j in range(m * JC, (m + 1) * JC):
-            rows = slice(j * 64, (j + 1) * 64)
-            gp[rows, 0:128], gp[rows, 128:256] = split(g_all[:, j].reshape(64, 128))
+        for jp in range(m * JC // 2, (m + 1) * JC // 2):
+            v = jnp.concatenate(
+                [g_all[:, 2 * jp].reshape(64, 128), g_all[:, 2 * jp + 1].reshape(64, 128)], axis=0
+            )
+            rows = slice(jp * 128, (jp + 1) * 128)
+            gp[rows, 0:128], gp[rows, 128:256] = split(v)
+            gt[0:128, rows], gt[128:256, rows] = split(v.T)
 
     def grad_outer(m):
         right = slice(m * JC * 64, (m + 1) * JC * 64)
@@ -231,11 +237,9 @@
         def make_d(n, _):
             for c2 in range(2):
                 rows = pl.ds(pl.multiple_of(n * 256 + c2 * 128, 128), 128)
-                v = lax.dot_general(
-                    wp[rows, 0:256], gp[right, :], CONTRACT_LANES, preferred_element_type=F32
-                ) + lax.dot_general(
-                    wp[rows, 128:384], gp[right, :], CONTRACT_LANES, preferred_element_type=F32
-                )
+                v = jnp.dot(
+                    wp[rows, 0:256], gt[:, right], preferred_element_type=F32
+                ) + jnp.dot(wp[rows, 128:384], gt[:, right], preferred_element_type=F32)
                 h, l = split(v)
                 for c in range(4):
                     lanes = pl.ds(pl.multiple_of(n * 1024 + (c2 * 4 + c) * 128, 128), 128)
@@ -313,32 +317,25 @@
     lax.fori_loop(8, 16, make_o, 0)
     forward(7)
 
-    for m in range(4):
-        if m:
-            prep_g(m)
-
-        def add_w(n, _):
-            rows = pl.ds(pl.multiple_of(n * 256, 256), 256)
-            lanes = slice(m * 512, (m + 1) * 512)
-            right = gp[m * 512 : (m + 1) * 512, :]
-            v = jnp.dot(o_h[rows, lanes], right, preferred_element_type=F32) + jnp.dot(
-                o_l[rows, lanes], right, preferred_element_type=F32
+    for m in range(1, 4):
+        prep_g(m)
+
+    def add_w(first):
+        def step(n, _):
+            rows = pl.ds(pl.multiple_of(first + n * 256, 256), 256)
+            gw = jnp.dot(o_h[rows, :], gp[...], preferred_element_type=F32) + jnp.dot(
+                o_l[rows, :], gp[...], preferred_element_type=F32
             )
-            if m:
-                v = v + acc_w[rows, :]
-            if m < 3:
-                acc_w[rows, :] = v
-            else:
-                gw_part[rows, :] = (v[:, 0:128] + v[:, 128:256]) * (1.0 / S)
+            gw_part[rows, :] = (gw[:, 0:128] + gw[:, 128:256]) * (1.0 / S)
             return 0
 
-        lax.fori_loop(0, 4, add_w, 0)
-
+        lax.fori_loop(0, 2, step, 0)
+
+    b_core = start(rcopy(bias_own, bias_r1, B_CORE, sibling))
+    add_w((1 - core) * 512)
     other = pl.ds(pl.multiple_of((1 - core) * 512, 512), 512)
     w_core = start(rcopy(gw_part.at[other], gw_r1, W_CORE, sibling))
-    b_core = start(rcopy(bias_own, bias_r1, B_CORE, sibling))
-
-    grad_outer(0)
+    add_w(core * 512)
     w_core.wait_recv()
     b_core.wait_recv()
     bias = bias_own[...] + bias_r1[...]
@@ -374,17 +371,8 @@
             jp = m * 4 + t
             bjs[jp * 64 : (jp + 1) * 64, 0:32] = v[:, t * 32 : (t + 1) * 32]
 
-    for m in range(1, 4):
+    for m in range(4):
         grad_outer(m)
-    for copy in w_xy:
-        copy.wait_recv()
-    v = gw_r2[0]
-    for n in range(1, 16):
-        v = v + gw_r2[n]
-    gw_z1[z % 4] = v
-    w_z1 = [
-        start(rcopy(gw_z1.at[z % 4], gw_z1.at[z % 4], W_Z1 + n, z_near[n])) for n in range(3)
-    ]
     def add_a(n, _):
         lanes = pl.ds(pl.multiple_of(n * 256, 256), 256)
         v = jnp.dot(bg[...], d_h[:, lanes], preferred_element_type=F32) + jnp.dot(
@@ -397,7 +385,17 @@
             acc_a[rows, :] = jnp.where(low_lanes, part[0:32], part[32:64])
         return 0
 
-    lax.fori_loop(0, 16, add_a, 0)
+    lax.fori_loop(0, 10, add_a, 0)
+    for copy in w_xy:
+        copy.wait_recv()
+    v = gw_r2[0]
+    for n in range(1, 16):
+        v = v + gw_r2[n]
+    gw_z1[z % 4] = v
+    w_z1 = [
+        start(rcopy(gw_z1.at[z % 4], gw_z1.at[z % 4], W_Z1 + n, z_near[n])) for n in range(3)
+    ]
+    lax.fori_loop(10, 16, add_a, 0)
     for core_ in range(2):
         for x_ in range(4):
             s0 = 4 * (x_ * 2 + core_)
@@ -407,12 +405,6 @@
             ga_all[core_, x_] = ((v[0:64] + v[64:128]) * (1.0 / S)).reshape(8, 8, 128)
     ga_core = start(rcopy(ga_all.at[1 - core], ga_r1, GA_CORE, sibling))
 
-    for copy in w_z1:
-        copy.wait_recv()
-    gw_z2[z // 4] = (gw_z1[0] + gw_z1[1]) + (gw_z1[2] + gw_z1[3])
-    w_z2 = [
-        start(rcopy(gw_z2.at[z // 4], gw_z2.at[z // 4], W_Z2 + n, z_far[n])) for n in range(3)
-    ]
     ga_core.wait_recv()
     for x_ in range(4):
         ga_r1[x_] = ga_r1[x_] + ga_all[core, x_]
@@ -421,8 +413,12 @@
     for n, d in enumerate((1, 2, 3)):
         ga_x.append(start(rcopy(ga_r1.at[(x + d) % 4], ga_r2.at[x], GA_X + n, x_peers[n])))
 
-    add_b(0)
-    add_b(1)
+    for copy in w_z1:
+        copy.wait_recv()
+    gw_z2[z // 4] = (gw_z1[0] + gw_z1[1]) + (gw_z1[2] + gw_z1[3])
+    w_z2 = [
+        start(rcopy(gw_z2.at[z // 4], gw_z2.at[z // 4], W_Z2 + n, z_far[n])) for n in range(3)
+    ]
     for copy in ga_x:
         copy.wait_recv()
     ga_s[...] = (ga_r2[0] + ga_r2[1]) + (ga_r2[2] + ga_r2[3])
@@ -443,6 +439,8 @@
 
     for d in range(1, 8):
         start(ga_z[d])
+    add_b(0)
+    add_b(1)
     for copy in w_z2:
         copy.wait_recv()
     v = (gw_z2[0] + gw_z2[1]) + (gw_z2[2] + gw_z2[3])
@@ -451,15 +449,18 @@
     w_ag = [
         start(rcopy(gw_out.at[mine], gw_out.at[mine], W_AG + n, xy_peers[n])) for n in range(15)
     ]
+    w_end = [start(rcopy(gw_out.at[mine], gw_out.at[mine], W_END + 15, sibling))]
     bias_out[...] = jnp.sum(v[32:40], axis=0, keepdims=True)
     add_b(2)
     add_b(3)
     for s in range(32):
         gb_out[:, s * 32 : (s + 1) * 32] = bjs[pl.ds(s, 32, stride=32), :][:, 0:32]
-    for copy in w_ag:
-        copy.wait_recv()
-    mine = gw_out.at[pl.ds(pl.multiple_of(core * 512, 512), 512)]
-    w_end = start(rcopy(mine, mine, W_END, sibling))
+    for n in reversed(range(15)):
+        w_ag[n].wait_recv()
+        dx, dy = xy_steps[n]
+        from_xy = ((x - dx) % 4) * 4 + (y - dy) % 4
+        part = gw_out.at[pl.ds(pl.multiple_of(core * 512 + from_xy * 32, 32), 32)]
+        w_end.append(start(rcopy(part, part, W_END + n, sibling)))
     for d in range(1, 8):
         ga_waits[d].wait_recv()
 
@@ -471,7 +472,8 @@
     for n in range(1, 8):
         v = v + ga_r3[n]
     ga_out[...] = v
-    w_end.wait_recv()
+    for copy in w_end:
+        copy.wait_recv()
     for copy in started:
         copy.wait_send()
 
@@ -526,6 +528,7 @@
             pltpu.VMEM((1024, 128), F32),
             pltpu.VMEM((256, 4096), BF16),
             pltpu.VMEM((2048, 256), BF16),
+            pltpu.VMEM((256, 2048), BF16),
             pltpu.VMEM((1024, 128), F32),
             pltpu.VMEM((1024, 256), F32),
             pltpu.VMEM((1024, 128), F32),

time: 83.8 us -> 82.8 us (0.988)
  no operation moved by 1% of the time
where the time goes in v3:
time: 82.8 us; the launch traced here: 82.7 us
  Pallas kernels  82 us (99%)
    pallas_call x1, Pallas kernels, local(): pl.pallas_call(kernel, out_shape=(jax.ShapeDtypeStruct((8, 128), F32), ja...  80 us
    pallas_call x1, Pallas kernels, local(): pl.pallas_call(hand_over, out_shape=tuple((jax.ShapeDtypeStruct(v.shape,...  1.98 us

profile of v3, /device:TPU:1, one launch (start us, length us, event | category | flops | bytes accessed | tf_op | source)
XLA Modules:
  0.0 82.7 jit_solution(9887135677425595845)
XLA Ops:
  0.6 80.0 %shard_map.75 = (f32[8,128]{1,0:T(8,128)}, f32[32,1024]{1,0:T(8,128)}, f32[1024,128]{1,0:T(8,128)}, f32[1,128]{1,0:T(1,128)}) custom-call(f32[8,128]{1,0:T(8,128)} %a_ref.1, f32[32,1024]{1,0:T(8,128)} %b_ref.1, f32[256,128]{1,0:T(8,128)} %bitcast.2, f32[1024,128]{1,0:T(8,128)} %w_ref.1), custom_call_target="tpu_custom_call" | custom-call | tf_op jit(solution)/shard_map/pallas_call | solution.py:494
  80.7 2.0 %shard_map.76 = (f32[8,128]{1,0:T(8,128)}, f32[32,1024]{1,0:T(8,128)}, f32[1024,128]{1,0:T(8,128)}, f32[1,128]{1,0:T(1,128)}) custom-call(f32[8,128]{1,0:T(8,128)} %get-tuple-element.12.refs_0_, f32[32,1024]{1,0:T(8,128)} %get-tuple-element.13.refs_1_, f32[1024,128]{1,0:T(8,128)} %get-tuple-element.14.refs_2_, f32[1,128]{1,0:T(1,128)} %get-tuple-element.15.refs_3_), custom_call_target="tpu_custom_call" | custom-call | tf_op jit(solution)/shard_map/pallas_call | solution.py:543
